TPU v7x, 32 devices: a whole 2x2x4 slice. The times are simulated.
32 devices in a mesh: seq: 16 (over z, x, core), blk: 2 (over y).
Axes of the slice: x: 2, y: 2, z: 4, core: 2. Of those that a mesh axis runs over, the one named last changes fastest.
Arguments:
- tokens: bfloat16 [16, 1024, 768], P('seq', 'blk'), may hold values from -6 to 6
- lengths: int32 [16, 4], P('seq'), may hold values from 32 to 768, as said below
- padding: int32 [16, 1024], P('seq', 'blk'), may hold values 0 or 1
- cotangent: bfloat16 [16, 1024, 768], P('seq', 'blk'), may hold values from -6 to 6
- ln1_gain: float32 [768], replicated, may hold values from 0.5 to 1.5
- ln1_bias: float32 [768], replicated, may hold values from -1 to 1
- w_qkv: bfloat16 [768, 2304], replicated, may hold values from -0.21875 to 0.21875
- q_bias: float32 [768], replicated, may hold values from -3 to 3
- v_bias: float32 [768], replicated, may hold values from -3 to 3
- w_out: bfloat16 [768, 768], replicated, may hold values from -6 to 6
- out_bias: float32 [768], replicated, may hold values from -2 to 2
- ln2_gain: float32 [768], replicated, may hold values from 0.5 to 1.5
- ln2_bias: float32 [768], replicated, may hold values from -1 to 1
- w_fc1: bfloat16 [768, 3072], replicated, may hold values from -0.21875 to 0.21875
- fc1_bias: float32 [3072], replicated, may hold values from -3 to 3
- w_fc2: bfloat16 [3072, 768], replicated, may hold values from -0.109375 to 0.109375
- fc2_bias: float32 [768], replicated, may hold values from -2 to 2
Outputs:
- result: bfloat16 [16, 1024, 768], P('seq', 'blk')
- grad_tokens: bfloat16 [16, 1024, 768], P('seq', 'blk')
- grad_ln1_gain: float32 [768], P(('seq', 'blk'))
- grad_ln1_bias: float32 [768], P(('seq', 'blk'))
- grad_w_qkv: float32 [768, 2304], P(('seq', 'blk'))
- grad_q_bias: float32 [768], P(('seq', 'blk'))
- grad_v_bias: float32 [768], P(('seq', 'blk'))
- grad_w_out: float32 [768, 768], P(('seq', 'blk'))
- grad_out_bias: float32 [768], P(('seq', 'blk'))
- grad_ln2_gain: float32 [768], P(('seq', 'blk'))
- grad_ln2_bias: float32 [768], P(('seq', 'blk'))
- grad_w_fc1: float32 [768, 3072], P(('seq', 'blk'))
- grad_fc1_bias: float32 [3072], P(('seq', 'blk'))
- grad_w_fc2: float32 [3072, 768], P(('seq', 'blk'))
- grad_fc2_bias: float32 [768], P(('seq', 'blk'))
Inputs may be any that keep to these rules, and one draw needn't show every extreme that they name: In each packed sequence the 4 clip lengths sum to 1024; one clip, a long video whose visible patches fill 1024 - 512 // 2 tokens, stands at a place drawn from the seed, and three short clips share the remaining 512 // 2.
All inputs are finite; a program needn't handle non-finite values. No bound on the sum of `padding` on one device may be relied on, other than what follows from the above.
Results may differ from a plain program's by a relative error of at most 0.014.
Values may be sent and summed in bfloat16 or wider, within the bound.
A program may use at most 256 MiB of HBM per device.

v0:
```python
import functools

import jax
import jax.numpy as jnp
from jax import lax
from jax.experimental import pallas as pl
from jax.experimental.pallas import tpu as pltpu
from jax.sharding import PartitionSpec as P

D = 768
FF = 3072
HEADS = 12
HEAD_DIM = 64


epsilon = 1e-06
score_scale = 0.125
masked_score = -1e30


def clip_numbers(clip_lengths, positions):
    bounds = jnp.cumsum(clip_lengths)
    return jnp.sum((positions[:, None] >= bounds[None, :]).astype(jnp.int32), axis=1)


def normalize(values, scales, offset):
    center = values - jnp.mean(values, axis=-1, keepdims=True)
    spread = jnp.mean(center * center, axis=-1, keepdims=True)
    inverse = lax.rsqrt(spread + epsilon)
    unit = center * inverse
    return (unit * scales + offset, unit, inverse)


def norm_back(upstream, unit, inverse, scales):
    scaled = upstream * scales
    return inverse * (
        scaled
        - jnp.mean(scaled, axis=-1, keepdims=True)
        - unit * jnp.mean(scaled * unit, axis=-1, keepdims=True)
    )


def gelu_slope(pre_gelu):
    cdf_part = 0.5 * (1.0 + lax.erf(pre_gelu * 0.7071067811865476))
    return cdf_part + pre_gelu * jnp.exp(-0.5 * pre_gelu * pre_gelu) * 0.3989422804014327


def masked_scores(query_heads, key_heads, clip_ids, positions, block_tags, key_pos):
    raw_scores = (
        jnp.einsum("qhd,khd->qhk", query_heads, key_heads, preferred_element_type=jnp.float32)
        * score_scale
    )
    allowed = (block_tags[None, :] == clip_ids[:, None]) | (positions[:, None] == key_pos[None, :])
    return jnp.where(allowed[:, None, :], raw_scores, masked_score)


def score_grads(
    query_heads,
    key_heads,
    value_heads,
    grad_heads,
    log_total,
    row_delta,
    clip_ids,
    positions,
    block_tags,
    key_pos,
):
    scores = masked_scores(query_heads, key_heads, clip_ids, positions, block_tags, key_pos)
    attn_probs = jnp.exp(scores - log_total[..., None])
    grad_probs = jnp.einsum(
        "qhd,khd->qhk", grad_heads, value_heads, preferred_element_type=jnp.float32
    )
    grad_scores = (attn_probs * (grad_probs - row_delta[..., None])).astype(jnp.bfloat16)
    return (attn_probs, grad_scores)


def stage_orders():
    seq_bits = lax.axis_size("seq").bit_length() - 1
    blk_bits = lax.axis_size("blk").bit_length() - 1
    seq_stages = [blk_bits + b for b in range(seq_bits)]
    blk_stages = list(range(blk_bits))
    one = seq_stages[:2] + blk_stages + seq_stages[2:]
    two = seq_stages[:1] + blk_stages + seq_stages[1:]
    return one, two


def scatter_stages(terms, order):
    n_dev = terms.shape[0]
    bits = n_dev.bit_length() - 1
    me = lax.axis_index("seq") * lax.axis_size("blk") + lax.axis_index("blk")
    rest = terms.shape[1:]
    kind = terms.dtype
    held = terms.reshape((2,) * bits + rest)
    for number, bit in enumerate(order):
        axis = bits - 1 - bit
        mine = (me >> bit) & 1
        sent = lax.dynamic_slice_in_dim(held, 1 - mine, 1, axis)
        kept = lax.dynamic_slice_in_dim(held, mine, 1, axis)
        swap = [(i, i ^ (1 << bit)) for i in range(n_dev)]
        came = lax.ppermute(sent, ("seq", "blk"), swap)
        total = kept.astype(jnp.float32) + came.astype(jnp.float32)
        held = total if number == bits - 1 else total.astype(kind)
    return held.reshape((1,) + rest)


def scatter_sum(grad):
    n_dev = lax.axis_size("seq") * lax.axis_size("blk")
    rows, width = grad.shape
    terms = grad.astype(jnp.bfloat16).reshape(n_dev, rows // n_dev, width)
    one, two = stage_orders()
    left = scatter_stages(terms[:, :, : width // 2], one)[0]
    right = scatter_stages(terms[:, :, width // 2 :], two)[0]
    return jnp.concatenate([left, right], axis=1)


def body(
    tokens,
    lengths,
    padding,
    cotangent,
    ln1_gain,
    ln1_bias,
    w_qkv,
    q_bias,
    v_bias,
    w_out,
    out_bias,
    ln2_gain,
    ln2_bias,
    w_fc1,
    fc1_bias,
    w_fc2,
    fc2_bias,
):
    tok_rows = tokens.shape[1]
    group_size = lax.axis_size("blk")
    n_dev = lax.axis_size("seq") * group_size
    positions = lax.axis_index("blk") * tok_rows + jnp.arange(tok_rows, dtype=jnp.int32)
    clip_ids = clip_numbers(lengths[0], positions)
    key_tags = jnp.where(padding[0] == 1, -1, clip_ids)
    tokens_f32 = tokens[0].astype(jnp.float32)
    first_norm, unit_one, inverse_one = normalize(tokens_f32, ln1_gain, ln1_bias)
    normed_one = first_norm.astype(jnp.bfloat16)
    joint_bias = jnp.concatenate([q_bias, jnp.zeros_like(q_bias), v_bias])
    projected = (
        jnp.dot(normed_one, w_qkv, preferred_element_type=jnp.float32) + joint_bias
    ).astype(jnp.bfloat16)
    keys_own = projected[:, D : 2 * D]
    values_own = projected[:, 2 * D :]
    query_heads = projected[:, :D].reshape(tok_rows, HEADS, HEAD_DIM)
    starts = jnp.arange(group_size, dtype=jnp.int32) * tok_rows

    def fold_keys(running, key_block, offset):
        block_keys, block_values, block_tags = key_block
        key_count = block_keys.shape[0]
        key_pos = offset + jnp.arange(key_count, dtype=jnp.int32)
        scores = masked_scores(
            query_heads,
            block_keys.reshape(key_count, HEADS, HEAD_DIM),
            clip_ids,
            positions,
            block_tags,
            key_pos,
        )
        row_max, row_sum, weighted = running
        new_max = jnp.maximum(row_max, jnp.max(scores, axis=-1))
        rescale = jnp.exp(row_max - new_max)
        exp_scores = jnp.exp(scores - new_max[..., None])
        row_sum = row_sum * rescale + jnp.sum(exp_scores, axis=-1)
        weighted = weighted * rescale[..., None] + jnp.einsum(
            "qhk,khd->qhd",
            exp_scores.astype(jnp.bfloat16),
            block_values.reshape(key_count, HEADS, HEAD_DIM),
            preferred_element_type=jnp.float32,
        )
        return (new_max, row_sum, weighted)

    start_state = (
        jnp.full((tok_rows, HEADS), masked_score, jnp.float32),
        jnp.zeros((tok_rows, HEADS), jnp.float32),
        jnp.zeros((tok_rows, HEADS, HEAD_DIM), jnp.float32),
    )
    group_keys, group_values, group_tags = (
        lax.all_gather(keys_own, "blk", axis=0, tiled=True),
        lax.all_gather(values_own, "blk", axis=0, tiled=True),
        lax.all_gather(key_tags, "blk", axis=0, tiled=True),
    )

    def scan_fold(running, scan_args):
        return (fold_keys(running, (scan_args[0], scan_args[1], scan_args[2]), scan_args[3]), None)

    final_state = lax.scan(
        scan_fold,
        start_state,
        (
            group_keys.reshape(group_size, tok_rows, D),
            group_values.reshape(group_size, tok_rows, D),
            group_tags.reshape(group_size, tok_rows),
            starts,
        ),
    )[0]
    row_max, row_sum, weighted = final_state
    mixed_f32 = weighted / row_sum[..., None]
    log_total = row_max + jnp.log(row_sum)
    mixed = mixed_f32.reshape(tok_rows, D).astype(jnp.bfloat16)
    residual = tokens_f32 + jnp.dot(mixed, w_out, preferred_element_type=jnp.float32) + out_bias
    second_norm, unit_two, inverse_two = normalize(residual, ln2_gain, ln2_bias)
    normed_two = second_norm.astype(jnp.bfloat16)
    pre_gelu = jnp.dot(normed_two, w_fc1, preferred_element_type=jnp.float32) + fc1_bias
    activated = jax.nn.gelu(pre_gelu, approximate=False).astype(jnp.bfloat16)
    result = (
        residual + jnp.dot(activated, w_fc2, preferred_element_type=jnp.float32) + fc2_bias
    ).astype(jnp.bfloat16)
    grad_out = cotangent[0]
    grad_fc2_bias = jnp.sum(grad_out, axis=0, dtype=jnp.float32)
    grad_w_fc2 = jnp.einsum("tf,td->fd", activated, grad_out, preferred_element_type=jnp.float32)
    grad_act = jnp.einsum("td,fd->tf", grad_out, w_fc2, preferred_element_type=jnp.float32)
    grad_pre = (grad_act * gelu_slope(pre_gelu)).astype(jnp.bfloat16)
    grad_fc1_bias = jnp.sum(grad_pre, axis=0, dtype=jnp.float32)
    grad_w_fc1 = jnp.einsum("td,tf->df", normed_two, grad_pre, preferred_element_type=jnp.float32)
    grad_norm_two = jnp.einsum("tf,df->td", grad_pre, w_fc1, preferred_element_type=jnp.float32)
    grad_ln2_gain = jnp.sum(grad_norm_two * unit_two, axis=0)
    grad_ln2_bias = jnp.sum(grad_norm_two, axis=0)
    grad_residual = grad_out.astype(jnp.float32) + norm_back(
        grad_norm_two, unit_two, inverse_two, ln2_gain
    )
    grad_branch = grad_residual.astype(jnp.bfloat16)
    grad_out_bias = jnp.sum(grad_branch, axis=0, dtype=jnp.float32)
    grad_w_out = jnp.einsum("td,te->de", mixed, grad_branch, preferred_element_type=jnp.float32)
    grad_mixed = jnp.einsum(
        "te,de->td", grad_branch, w_out, preferred_element_type=jnp.float32
    ).astype(jnp.bfloat16)
    grad_heads = grad_mixed.reshape(tok_rows, HEADS, HEAD_DIM)
    row_delta = jnp.sum(grad_heads * mixed_f32, axis=-1)
    key_stack = (
        group_keys.reshape(group_size, tok_rows, D),
        group_values.reshape(group_size, tok_rows, D),
        group_tags.reshape(group_size, tok_rows),
        starts,
    )

    def back_block(grad_queries, scan_args):
        block_keys, block_values, block_tags, offset = scan_args
        key_pos = offset + jnp.arange(tok_rows, dtype=jnp.int32)
        key_heads = block_keys.reshape(tok_rows, HEADS, HEAD_DIM)
        value_heads = block_values.reshape(tok_rows, HEADS, HEAD_DIM)
        attn_probs, grad_scores = score_grads(
            query_heads,
            key_heads,
            value_heads,
            grad_heads,
            log_total,
            row_delta,
            clip_ids,
            positions,
            block_tags,
            key_pos,
        )
        grad_values = jnp.einsum(
            "qhk,qhd->khd",
            attn_probs.astype(jnp.bfloat16),
            grad_heads,
            preferred_element_type=jnp.float32,
        )
        grad_queries = (
            grad_queries
            + jnp.einsum("qhk,khd->qhd", grad_scores, key_heads, preferred_element_type=jnp.float32)
            * score_scale
        )
        grad_keys = (
            jnp.einsum("qhk,qhd->khd", grad_scores, query_heads, preferred_element_type=jnp.float32)
            * score_scale
        )
        return (
            grad_queries,
            jnp.concatenate(
                [grad_keys.reshape(tok_rows, D), grad_values.reshape(tok_rows, D)], axis=1
            ),
        )

    grad_queries, key_terms = lax.scan(
        back_block, jnp.zeros((tok_rows, HEADS, HEAD_DIM), jnp.float32), key_stack
    )
    key_sums = lax.psum_scatter(
        key_terms.reshape(group_size * tok_rows, 2 * D).astype(jnp.bfloat16),
        "blk",
        scatter_dimension=0,
        tiled=True,
    )
    grad_qkv = jnp.concatenate(
        [grad_queries.reshape(tok_rows, D).astype(jnp.bfloat16), key_sums], axis=1
    )
    grad_q_bias = jnp.sum(grad_qkv[:, :D], axis=0, dtype=jnp.float32)
    grad_v_bias = jnp.sum(grad_qkv[:, 2 * D :], axis=0, dtype=jnp.float32)
    grad_w_qkv = jnp.einsum("td,te->de", normed_one, grad_qkv, preferred_element_type=jnp.float32)
    grad_norm_one = jnp.einsum("te,de->td", grad_qkv, w_qkv, preferred_element_type=jnp.float32)
    grad_ln1_gain = jnp.sum(grad_norm_one * unit_one, axis=0)
    grad_ln1_bias = jnp.sum(grad_norm_one, axis=0)
    grad_tokens = (
        grad_residual + norm_back(grad_norm_one, unit_one, inverse_one, ln1_gain)
    ).astype(jnp.bfloat16)
    small = jnp.concatenate(
        [
            v.reshape(n_dev, -1)
            for v in (
                grad_ln1_gain,
                grad_ln1_bias,
                grad_q_bias,
                grad_v_bias,
                grad_out_bias,
                grad_ln2_gain,
                grad_ln2_bias,
                grad_fc1_bias,
                grad_fc2_bias,
            )
        ],
        axis=1,
    )
    sum_fc2 = scatter_sum(grad_w_fc2)
    sum_fc1 = scatter_sum(grad_w_fc1)
    sum_out = scatter_sum(grad_w_out)
    sum_qkv = scatter_sum(grad_w_qkv)
    part = D // n_dev
    small = scatter_stages(small, stage_orders()[0])[0]
    pieces = []
    at = 0
    for size in (part, part, part, part, part, part, part, FF // n_dev, part):
        pieces.append(small[at : at + size])
        at += size
    summed = (
        pieces[0],
        pieces[1],
        sum_qkv,
        pieces[2],
        pieces[3],
        sum_out,
        pieces[4],
        pieces[5],
        pieces[6],
        sum_fc1,
        pieces[7],
        sum_fc2,
        pieces[8],
    )
    return (
        result[None],
        grad_tokens[None],
        summed[0],
        summed[1],
        summed[2],
        summed[3],
        summed[4],
        summed[5],
        summed[6],
        summed[7],
        summed[8],
        summed[9],
        summed[10],
        summed[11],
        summed[12],
    )


f32 = jnp.float32
bf16 = jnp.bfloat16
MESH = pl.DeviceIdType.MESH
PAIRS = HEADS // 2
FF_CHUNK = 512
ROW_TILE = 128
TWIN_UNROLL = 1
ITEMS = 18
ITEM_ROWS = 512
ITEM_LANES = 768
SLOTS = 6
STAGES = 5
STARTS = (0, 1, 2, 3, 4, 5, 7, 8, 9, 10, 11, 12, 15, 16, 17, 18, 19, 20)
ENDS = (0, 1, 4, 7, 10, 13)
SUMS_AT = (1, 3, 6, 9, 12)
LANDING = (0, 256, 384, 448, 480)
LANDING_ROWS = 496
FLAT_BITS = ("y", "c", "x", "z0", "z1")
GROUPS = (
    (("c", "x", "y", "z0", "z1"), 0, 512),
    (("c", "z0", "z1", "y", "x"), 512, 256),
)


def fits(mesh):
    return dict(mesh.shape) == {"seq": 16, "blk": 2}


def dot(a, b):
    return lax.dot_general(a, b, (((1,), (0,)), ((), ())), preferred_element_type=f32)


def dot_nt(a, b):
    return lax.dot_general(a, b, (((1,), (1,)), ((), ())), preferred_element_type=f32)


def dot_tn(a, b):
    return lax.dot_general(a, b, (((0,), (0,)), ((), ())), preferred_element_type=f32)


def aligned(at, step):
    return at if isinstance(at, int) else pl.multiple_of(at, step)


def unit_of(values):
    center = values - jnp.mean(values, axis=1, keepdims=True)
    inverse = lax.rsqrt(jnp.mean(center * center, axis=1, keepdims=True) + epsilon)
    return center * inverse, inverse


def row(ref):
    return ref[...].reshape(1, ref.shape[0])


def column_sum(values):
    return jnp.sum(values, axis=0, keepdims=True)


def block_kernel(
    tok_hbm,
    len_ref,
    pad_ref,
    cot_hbm,
    ln1_gain,
    ln1_bias,
    wqkv_hbm,
    q_bias,
    v_bias,
    wout_hbm,
    out_bias,
    ln2_gain,
    ln2_bias,
    wfc1_hbm,
    fc1_bias,
    wfc2_hbm,
    fc2_bias,
    result_hbm,
    gtok_hbm,
    out_ln1g,
    out_ln1b,
    out_qkv,
    out_qb,
    out_vb,
    out_out,
    out_ob,
    out_ln2g,
    out_ln2b,
    out_fc1,
    out_fb1,
    out_fc2,
    out_fb2,
    e_hbm,
    wqkv,
    wout,
    wfc1,
    tok,
    tokp,
    cot,
    nrm,
    unit_t,
    nrm2_t,
    qkv,
    kvp,
    gm,
    bias,
    ering,
    slots,
    terms,
    landing,
    gn_in,
    tags,
    vec_ref,
    fb1_ref,
    small,
    small_in,
    cs_ref,
    cs_in,
    load_sem,
    e_sem,
    send_sem,
    recv_sem,
    item_send,
    item_recv,
    small_send,
    small_recv,
    sums_send,
    sums_recv,
):
    rows = tok.shape[0]
    seq = lax.axis_index("seq")
    blk = lax.axis_index("blk")
    bit = {
        "y": blk,
        "c": lax.rem(seq, 2),
        "x": lax.rem(seq // 2, 2),
        "z0": lax.rem(seq // 4, 2),
        "z1": seq // 8,
    }
    across = {
        "y": (seq, 1 - blk),
        "c": (seq + 1 - 2 * bit["c"], blk),
        "x": (seq + 2 - 4 * bit["x"], blk),
        "z0": (seq + 4 - 8 * bit["z0"], blk),
        "z1": (seq + 8 - 16 * bit["z1"], blk),
    }
    twin = across["y"]

    barrier = pltpu.get_barrier_semaphore()
    for name in FLAT_BITS:
        pl.semaphore_signal(barrier, inc=1, device_id=across[name], device_id_type=MESH)

    wfc2_at = (ITEMS - 6) * ITEM_ROWS
    wfc2 = terms.at[pl.ds(wfc2_at, FF)]
    loads = [
        pltpu.make_async_copy(src, dst, load_sem.at[i])
        for i, (src, dst) in enumerate(
            (
                (tok_hbm.at[0], tok),
                (wqkv_hbm, wqkv),
                (wout_hbm, wout),
                (wfc1_hbm, wfc1),
                (wfc2_hbm, wfc2),
                (cot_hbm.at[0], cot),
            )
        )
    ]
    for copy in loads:
        copy.start()

    ends = []
    total = jnp.int32(0)
    for i in range(len_ref.shape[1]):
        total = total + len_ref[0, i]
        ends.append(total)

    def clips_at(positions):
        number = jnp.zeros_like(positions)
        for end in ends:
            number = number + jnp.where(positions >= end, 1, 0)
        return number

    base = blk * rows
    lane_pos = base + lax.broadcasted_iota(jnp.int32, (8, rows), 1)
    padding = jnp.broadcast_to(pad_ref[...], (8, rows))
    tags[0] = jnp.where(padding == 1, -1, clips_at(lane_pos))

    pl.semaphore_wait(barrier, len(FLAT_BITS))

    def to_twin(i, src, dst):
        return pltpu.make_async_remote_copy(
            src_ref=src,
            dst_ref=dst,
            send_sem=send_sem.at[i],
            recv_sem=recv_sem.at[i],
            device_id=twin,
            device_id_type=MESH,
        )

    part_rows = rows // 2
    send_tags = to_twin(1, tags.at[0], tags.at[1])
    send_tags.start()
    send_tok = []
    for part, sem in ((0, 0), (1, 8)):
        here = pl.ds(part * part_rows, part_rows)
        send_tok.append(to_twin(sem, tok_hbm.at[0, here], tokp.at[here]))
        send_tok[part].start()

    def place_of(order, there):
        at = 0
        for stage, name in enumerate(order):
            differs = there[name] + bit[name] - 2 * there[name] * bit[name]
            at = at + (16 >> stage) * differs
        return at

    def bits_of(d):
        return {name: (d >> i) & 1 for i, name in enumerate(FLAT_BITS)}

    def item_copies(stage, item):
        count = ITEM_ROWS >> stage
        slot = item % SLOTS if isinstance(item, int) else lax.rem(item, SLOTS)
        first = item * ITEM_ROWS
        src_at = aligned(first + count, 16)
        dst_at = aligned(slot * LANDING_ROWS + LANDING[stage - 1], 16)
        copies = []
        for group, (order, lane, width) in enumerate(GROUPS):
            if stage == 1:
                if group > 0:
                    break
                width = ITEM_LANES
            lanes = pl.ds(lane, width)
            sem = (slot * STAGES + stage - 1) * len(GROUPS) + group
            copies.append(
                pltpu.make_async_remote_copy(
                    src_ref=terms.at[pl.ds(src_at, count), lanes],
                    dst_ref=landing.at[pl.ds(dst_at, count), lanes],
                    send_sem=item_send.at[sem],
                    recv_sem=item_recv.at[sem],
                    device_id=across[order[stage - 1]],
                    device_id_type=MESH,
                )
            )
        return copies

    def start_stage(stage, item):
        for copy in item_copies(stage, item):
            copy.start()

    def store_sum(item, kind, values):
        if kind == 1:
            at = aligned((item - 6) * 16, 16)
            out_fc2[pl.ds(at, 16), :] = values
            return
        parts = (
            (0, 16, values[:, :256], values[:, 256:512]),
            (16, 8, values[:8, 512:], values[8:, 512:]),
        )
        for top, count, left, right in parts:
            here = pl.ds(top, count)
            if kind == 0:
                col = aligned(item * 512, 512)
                out_fc1[here, pl.ds(col, 256)] = left
                out_fc1[here, pl.ds(col + 256, 256)] = right
            else:
                col = aligned((item - 12) * 128, 128)
                out_qkv[here, pl.ds(D + col, 128)] = left[:, :128]
                out_qkv[here, pl.ds(2 * D + col, 128)] = left[:, 128:]
                out_qkv[here, pl.ds(col, 128)] = right[:, :128]
                out_out[here, pl.ds(col, 128)] = right[:, 128:]

    def finish_stage(stage, item, low, high):
        for copy in item_copies(stage, item):
            copy.wait()
        count = ITEM_ROWS >> stage
        slot = item % SLOTS if isinstance(item, int) else lax.rem(item, SLOTS)
        first = item * ITEM_ROWS
        here = pl.ds(aligned(first, 16), count)
        came = pl.ds(aligned(slot * LANDING_ROWS + LANDING[stage - 1], 16), count)
        if stage < STAGES:
            terms[here, :] = terms[here, :] + landing[came, :]
            start_stage(stage + 1, item)
            return
        values = terms[here, :].astype(f32) + landing[came, :].astype(f32)
        for kind in range(3):
            if high < 6 * kind or low >= 6 * kind + 6:
                continue
            if low >= 6 * kind and high < 6 * kind + 6:
                store_sum(item, kind, values)
            else:
                pl.when((item >= 6 * kind) & (item < 6 * kind + 6))(
                    functools.partial(store_sum, item, kind, values)
                )

    def feed_tick(number):
        for stage in range(STAGES, 0, -1):
            if ENDS[stage] < 6:
                item = number - ENDS[stage]
                act = functools.partial(finish_stage, stage, item, 0, 5)
                pl.when(item >= 0)(act)
        start_stage(1, number)

    def tick(number, low=None, high=None):
        low = number if low is None else low
        high = number if high is None else high
        for stage in range(STAGES, -1, -1):
            begun = range(low - ENDS[stage], high - ENDS[stage] + 1)
            items = [STARTS.index(t) for t in begun if t in STARTS]
            if not items:
                continue
            if low == high:
                item = items[0]
            else:
                t = number - ENDS[stage]
                item = t - jnp.where(t >= 7, 1, 0) - jnp.where(t >= 15, 2, 0)
            if stage == 0:
                act = functools.partial(start_stage, 1, item)
            else:
                act = functools.partial(finish_stage, stage, item, items[0], items[-1])
            if len(items) == len(begun):
                act()
            else:
                valid = None
                for t_out in begun:
                    if t_out not in STARTS:
                        here = t != t_out
                        valid = here if valid is None else valid & here
                pl.when(valid)(act)

    def put_24(item, values):
        base_row = item * ITEM_ROWS
        for d in range(32):
            top = values[24 * d : 24 * d + 16, :]
            rest = values[24 * d + 16 : 24 * d + 24, :]
            rest = jnp.concatenate([rest[:, :256], rest[:, 256:]], axis=0)
            block = jnp.concatenate([top, rest], axis=1).astype(bf16)
            for order, lane, width in GROUPS:
                at = pl.multiple_of(base_row + 16 * place_of(order, bits_of(d)), 16)
                terms[pl.ds(at, 16), lane : lane + width] = block[:, lane : lane + width]

    row_tiles = rows // ROW_TILE

    def tile(t):
        return pl.ds(pl.multiple_of(t * ROW_TILE, ROW_TILE), ROW_TILE)

    def first_norm(src, columns_at, first, last):
        gain, offset = row(ln1_gain), row(ln1_bias)

        def step(t, carry):
            unit, _ = unit_of(src[tile(t), :].astype(f32))
            normed = (unit * gain + offset).astype(bf16)
            nrm[tile(t), :] = normed
            at = pl.multiple_of(columns_at + t * ROW_TILE, ROW_TILE)
            unit_t[:, pl.ds(at, ROW_TILE)] = unit.astype(bf16).T
            return carry

        lax.fori_loop(first, last, step, 0)

    def set_bias(own, first, count):
        clip_col = clips_at(base + lax.broadcasted_iota(jnp.int32, (rows, count), 0))
        tag_row = tags[0 if own else 1, 0:1, first : first + count]
        allowed = jnp.broadcast_to(tag_row, (rows, count)) == clip_col
        if own:
            here = lax.broadcasted_iota(jnp.int32, (rows, count), 0)
            there = lax.broadcasted_iota(jnp.int32, (rows, count), 1)
            allowed = allowed | (here == there)
        bias[:, :count] = jnp.where(allowed, 0.0, masked_score)

    loads[0].wait()
    first_norm(tok, 0, 0, row_tiles)
    set_bias(True, 0, rows)
    loads[1].wait()
    wide = 256

    def project(kind, add, scale, dst, dst_at, first=0, count=rows):
        here = pl.ds(first, count)

        def step(c, carry):
            col = pl.multiple_of(c * wide, wide)
            out = dot(nrm[here, :], wqkv[:, pl.ds(kind * D + col, wide)])
            if add is not None:
                out = out + add[pl.ds(col, wide)].reshape(1, wide)
            out = out.astype(bf16)
            if scale:
                out = out * jnp.bfloat16(score_scale)
            dst[here, pl.ds(dst_at + col, wide)] = out
            return carry

        lax.fori_loop(0, D // wide, step, 0)

    project(0, q_bias, True, qkv, 0)
    project(1, None, False, qkv, D)
    project(2, v_bias, False, qkv, 2 * D)

    low_lane = lax.broadcasted_iota(jnp.int32, (rows, 128), 1) < 64

    def half(values, h):
        mask = low_lane[: values.shape[0]]
        return jnp.where(mask if h == 0 else ~mask, values, jnp.zeros_like(values))

    def half_and_ones(values, h):
        return jnp.concatenate([half(values, h), half(jnp.ones_like(values), h)], axis=1)

    def e_out(hp):
        return pltpu.make_async_copy(ering.at[hp], e_hbm.at[hp], e_sem.at[hp])

    def e_in(hp):
        return pltpu.make_async_copy(e_hbm.at[hp], ering.at[hp], e_sem.at[hp])

    MIXED, F_OWN, F_A, F_B, RES, ACC, GNT = range(7)

    S_OWN, S_A, O_A = F_B, ACC, RES

    def forward_pair(part, hp):
        own = part == 0
        count = rows if own else part_rows
        first = 0 if own else (part - 1) * part_rows
        keys = pl.ds(first, count)
        ref, key_at, value_at = (qkv, D, 2 * D) if own else (kvp, 0, D)
        col = aligned(hp * 128, 128)
        cols = pl.ds(col, 128)
        q = qkv[:, cols]
        k = ref[keys, pl.ds(key_at + col, 128)]
        v = ref[keys, pl.ds(value_at + col, 128)]
        outs, tops = [], []
        for h in range(2):
            scores = dot_nt(q, half(k, h)) + bias[:, :count]
            top = jnp.max(scores, axis=1, keepdims=True)
            e = jnp.exp(scores - top).astype(bf16)
            ering[hp, h, :, first : first + count] = e
            outs.append(dot(e, half_and_ones(v, h)))
            tops.append(top)
        both_heads = outs[0] + outs[1]
        weighted, sums = both_heads[:, :128], both_heads[:, 128:]
        top = jnp.where(low_lane, tops[0], tops[1])
        if part == 0:
            slots[MIXED, :, cols] = weighted
            slots[S_OWN, :, cols] = sums
            slots[F_OWN, :, cols] = top
            return
        if part == 1:
            slots[O_A, :, cols] = weighted
            slots[S_A, :, cols] = sums
            slots[F_A, :, cols] = top
            return
        top_own, top_a = slots[F_OWN, :, cols], slots[F_A, :, cols]
        highest = jnp.maximum(jnp.maximum(top_own, top_a), top)
        w_own = jnp.exp(top_own - highest)
        w_a = jnp.exp(top_a - highest)
        w_b = jnp.exp(top - highest)
        inverse = 1.0 / (w_own * slots[S_OWN, :, cols] + w_a * slots[S_A, :, cols] + w_b * sums)
        w_own, w_a, w_b = w_own * inverse, w_a * inverse, w_b * inverse
        slots[MIXED, :, cols] = (
            w_own * slots[MIXED, :, cols] + w_a * slots[O_A, :, cols] + w_b * weighted
        )
        slots[F_OWN, :, cols] = w_own
        slots[F_A, :, cols] = w_a
        slots[F_B, :, cols] = w_b

    def forward_three(part):
        def step(i, carry):
            for p in range(3):
                forward_pair(part, 3 * i + p)
            if part == 0:
                for p in range(3):
                    e_out(3 * i + p).start()
            return carry

        lax.fori_loop(0, PAIRS // 3, step, 0)

    forward_three(0)

    send_tags.wait()
    for part in (1, 2):
        first = (part - 1) * part_rows
        send_tok[part - 1].wait()
        first_norm(tokp, rows, first // ROW_TILE, (first + part_rows) // ROW_TILE)
        set_bias(False, first, part_rows)
        project(1, None, False, kvp, 0, first, part_rows)
        project(2, v_bias, False, kvp, D, first, part_rows)
        if part == 1:
            for hp in range(PAIRS):
                e_out(hp).wait()
        forward_three(part)

    loads[2].wait()

    def branch(c, carry):
        cols = pl.ds(pl.multiple_of(c * wide, wide), wide)
        out = dot(slots[MIXED].astype(bf16), wout[:, cols])
        out = out + out_bias[cols].reshape(1, wide)
        slots[RES, :, cols] = tok[:, cols].astype(f32) + out
        return carry

    lax.fori_loop(0, D // wide, branch, 0)
    gain_two, offset_two = row(ln2_gain), row(ln2_bias)

    def second_norm(t, carry):
        unit, _ = unit_of(slots[RES, tile(t), :])
        normed = (unit * gain_two + offset_two).astype(bf16)
        nrm[tile(t), :] = normed
        nrm2_t[:, tile(t)] = normed.T
        slots[ACC, tile(t), :] = jnp.zeros((ROW_TILE, D), f32)
        slots[GNT, tile(t), :] = jnp.zeros((ROW_TILE, D), f32)
        return carry

    lax.fori_loop(0, row_tiles, second_norm, 0)

    loads[3].wait()
    loads[4].wait()
    loads[5].wait()

    def feed(c, carry):
        units = pl.ds(pl.multiple_of(c * FF_CHUNK, FF_CHUNK), FF_CHUNK)
        w1 = wfc1[:, units]
        w2 = terms[pl.ds(pl.multiple_of(wfc2_at + c * FF_CHUNK, FF_CHUNK), FF_CHUNK), :]
        pre = dot(nrm[...], w1) + fc1_bias[units].reshape(1, FF_CHUNK)
        phi = 0.5 * (1.0 + lax.erf(pre * 0.7071067811865476))
        slope = phi + pre * jnp.exp(-0.5 * pre * pre) * 0.3989422804014327
        activated = (pre * phi).astype(bf16)
        grad_pre = (dot_nt(cot[...], w2) * slope).astype(bf16)
        slots[ACC] += dot(activated, w2)
        slots[GNT] += dot_nt(grad_pre, w1)
        @pl.when(c < 4)
        def _():
            wqkv[:rows, units] = activated

        @pl.when(c == 4)
        def _():
            wqkv[:rows, 8 * wide : 9 * wide] = activated[:, :wide]
            gm[:, :wide] = activated[:, wide:]

        @pl.when(c == 5)
        def _():
            gm[:, wide:] = activated

        fb1_ref[0:1, units] = column_sum(grad_pre.astype(f32))
        put_24(c, dot(nrm2_t[...], grad_pre))
        feed_tick(c)
        return carry

    lax.fori_loop(0, FF // FF_CHUNK, feed, 0)

    def weight_fc2(c, activated):
        values = jnp.concatenate(
            [dot_tn(activated[:, p * wide : (p + 1) * wide], cot[...]) for p in range(3)], axis=0
        )
        for low in range(8):
            there = bits_of(low)
            there["z0"], there["z1"] = (c % 2, c // 2) if isinstance(c, int) else (lax.rem(c, 2), c // 2)
            for order, lane, width in GROUPS:
                place = 16 * place_of(order, there)
                for j in range(6):
                    top = 96 * low + 16 * j
                    block = values[top : top + 16, lane : lane + width].astype(bf16)
                    at = pl.multiple_of((6 + j) * ITEM_ROWS + place, 16)
                    terms[pl.ds(at, 16), lane : lane + width] = block

    def weight_fc2_step(c, carry):
        weight_fc2(c, wqkv[:rows, pl.ds(pl.multiple_of(c * D, D), D)])
        return carry

    lax.fori_loop(0, 3, weight_fc2_step, 0)
    tick(6)
    weight_fc2(3, gm[...])
    reload = pltpu.make_async_copy(wqkv_hbm, wqkv, load_sem.at[1])
    reload.start()
    tick(7)

    vec_ref[...] = jnp.zeros(vec_ref.shape, f32)
    fb1_ref[1:8, :] = jnp.zeros((7, FF), f32)
    V_OB, V_LN2G, V_LN2B, V_FC2B = range(4)
    cs_ref[0] = jnp.zeros(cs_ref.shape[1:], f32)

    def add_vec(kind, values):
        vec_ref[kind : kind + 1, :] += column_sum(values)

    def second_back(t, carry):
        here = tile(t)
        unit, inverse = unit_of(slots[RES, here, :])
        tokp[here, :] = (
            slots[RES, here, :] + slots[ACC, here, :] + row(fc2_bias)
        ).astype(bf16)
        upstream = slots[GNT, here, :]
        grad_out = cot[here, :].astype(f32)
        add_vec(V_FC2B, grad_out)
        add_vec(V_LN2G, upstream * unit)
        add_vec(V_LN2B, upstream)
        scaled = upstream * gain_two
        grad = grad_out + inverse * (
            scaled
            - jnp.mean(scaled, axis=1, keepdims=True)
            - unit * jnp.mean(scaled * unit, axis=1, keepdims=True)
        )
        slots[RES, here, :] = grad
        low = grad.astype(bf16)
        nrm[here, :] = low
        add_vec(V_OB, low.astype(f32))
        return carry

    lax.fori_loop(0, 2, second_back, 0)
    tick(8)
    lax.fori_loop(2, row_tiles, second_back, 0)
    store_result = pltpu.make_async_copy(tokp, result_hbm.at[0], load_sem.at[0])
    store_result.start()
    tick(9)

    GQ = ACC

    def mixed_back(c, carry):
        cols = pl.ds(pl.multiple_of(c * wide, wide), wide)
        gm[:, cols] = dot_nt(nrm[...], wout[cols, :]).astype(bf16)
        mixed = slots[MIXED, :, cols].astype(bf16)
        wfc1[cols, :D] = dot_tn(mixed, nrm[...]).astype(bf16)
        return carry

    lax.fori_loop(0, D // wide, mixed_back, 0)
    def window(ref, first, count):
        block = first // 128 * 128
        shift = first - block
        wide_enough = 256 if shift + count > 128 else 128
        piece = ref[:, block : block + wide_enough]
        if shift:
            piece = pltpu.roll(piece, wide_enough - shift, 1)
        return piece[:, :128]

    small_order = GROUPS[0][0]
    for d in range(32):
        at = pl.multiple_of(16 * place_of(small_order, bits_of(d)), 16)
        small[pl.ds(at, 8), :] = window(vec_ref, 24 * d, 24)
        small[pl.ds(at + 8, 8), :] = window(fb1_ref, 96 * d, 96)

    def small_copy(stage):
        count = ITEM_ROWS >> stage
        return pltpu.make_async_remote_copy(
            src_ref=small.at[pl.ds(count, count)],
            dst_ref=small_in.at[pl.ds(LANDING[stage - 1], count)],
            send_sem=small_send.at[stage - 1],
            recv_sem=small_recv.at[stage - 1],
            device_id=across[small_order[stage - 1]],
            device_id_type=MESH,
        )

    def small_step(stage):
        small_copy(stage).wait()
        count = ITEM_ROWS >> stage
        came = small_in[LANDING[stage - 1] : LANDING[stage - 1] + count]
        small[:count] = small[:count] + came
        if stage < STAGES:
            small_copy(stage + 1).start()
            return
        for kind, ref in enumerate((out_ob, out_ln2g, out_ln2b, out_fb2)):
            ref[...] = small[kind, :24]
        out_fb1[...] = small[8, :96]

    small_copy(1).start()

    def sums_copy(stage):
        return pltpu.make_async_remote_copy(
            src_ref=cs_ref.at[stage - 1],
            dst_ref=cs_in.at[stage - 1],
            send_sem=sums_send.at[stage - 1],
            recv_sem=sums_recv.at[stage - 1],
            device_id=across[small_order[stage - 1]],
            device_id_type=MESH,
        )

    def sums_step(stage):
        sums_copy(stage).wait()
        cs_ref[stage] = cs_ref[stage - 1] + cs_in[stage - 1]
        if stage < STAGES:
            sums_copy(stage + 1).start()

    tick(10)

    def backward_pair(part, hp):
        own = part == 0
        ref, key_at, value_at = (qkv, D, 2 * D) if own else (kvp, 0, D)
        kind = (F_OWN, F_A, F_B)[part]
        count = rows if own else part_rows
        first = 0 if own else (part - 1) * part_rows
        keys = pl.ds(first, count)
        col = aligned(hp * 128, 128)
        cols = pl.ds(col, 128)
        q = qkv[:, cols]
        q_t = q.T
        k = ref[keys, pl.ds(key_at + col, 128)]
        v = ref[keys, pl.ds(value_at + col, 128)]
        grad_in = gm[:, cols].astype(f32)
        scaled = grad_in * slots[kind, :, cols]
        weighted = scaled * slots[MIXED, :, cols]
        scaled = scaled.astype(bf16)
        scaled_t = scaled.T
        grad_q = None
        grad_k, grad_v = [], []
        for h in range(2):
            delta = jnp.sum(half(weighted, h), axis=1, keepdims=True)
            e = ering[hp, h, :, first : first + count]
            grad_probs = dot_nt(scaled, half(v, h))
            grad_scores = (e.astype(f32) * (grad_probs - delta)).astype(bf16)
            term = dot(grad_scores, half(k, h))
            grad_q = term if grad_q is None else grad_q + term
            grad_k.append(dot(q_t[64 * h : 64 * h + 64], grad_scores))
            grad_v.append(dot(scaled_t[64 * h : 64 * h + 64], e))
        grad_k = jnp.concatenate(grad_k, axis=0).T.astype(bf16)
        grad_v = jnp.concatenate(grad_v, axis=0).T.astype(bf16)
        ref[keys, pl.ds(key_at + col, 128)] = grad_k
        ref[keys, pl.ds(value_at + col, 128)] = grad_v
        if part == 1:
            slots[GQ, :, cols] = grad_q
        elif part == 2:
            slots[GQ, :, cols] += grad_q
        else:
            total_q = (slots[GQ, :, cols] + grad_q) * score_scale
            qkv[:, cols] = total_q.astype(bf16)

    store_result.wait()
    reload.wait()
    send_gn = []
    for part in (1, 2):
        first = (part - 1) * part_rows
        here = pl.ds(first, part_rows)

        def twin_step(i, carry):
            for p in range(TWIN_UNROLL):
                backward_pair(part, TWIN_UNROLL * i + p)

            @pl.when(i == PAIRS // TWIN_UNROLL // 2 - 1)
            def _():
                tick(2 * part + 9)

            return carry

        lax.fori_loop(0, PAIRS // TWIN_UNROLL, twin_step, 0)
        if part == 2:
            for hp in range(PAIRS):
                e_in(hp).start()

        def partial_out(c, carry):
            cols = pl.ds(pl.multiple_of(c * wide, wide), wide)
            tokp[here, cols] = dot_nt(kvp[here, :], wqkv[cols, D : 3 * D]).astype(bf16)
            return carry

        lax.fori_loop(0, D // wide, partial_out, 0)
        for c in range(3):
            cols = pl.ds(wide * c, wide)
            sem = 2 + 3 * (part - 1) + c
            send_gn.append(to_twin(sem, tokp.at[here, cols], gn_in.at[here, cols]))
        tick(2 * part + 10)
        send_gn[part - 1].start()
        small_step(part)

    def own_step(hp, carry):
        e_in(hp).wait()
        backward_pair(0, hp)
        col = pl.multiple_of(hp * 128, 128)
        grad_q = qkv[:, pl.ds(col, 128)]
        own = jnp.concatenate(
            [qkv[:, pl.ds(D + col, 128)], qkv[:, pl.ds(2 * D + col, 128)]], axis=1
        )
        other = jnp.concatenate(
            [kvp[:, pl.ds(col, 128)], kvp[:, pl.ds(D + col, 128)]], axis=1
        )
        sum_kv = column_sum(own.astype(f32) + other.astype(f32))
        cs_ref[0, 0:1, pl.ds(col, 128)] = column_sum(grad_q.astype(f32))
        cs_ref[0, 1:2, pl.ds(col, 128)] = sum_kv[:, :128]
        cs_ref[0, 2:3, pl.ds(col, 128)] = sum_kv[:, 128:]
        weight_kv = dot(unit_t[...], jnp.concatenate([own, other], axis=0))
        weight_q = dot(unit_t[:, :rows], grad_q)
        weight_o = wfc1[:, pl.ds(col, 128)].astype(f32)
        put_24(12 + hp, jnp.concatenate([weight_kv, weight_q, weight_o], axis=1))
        tick(15 + hp, 15, 20)
        for c in range(4):
            pl.when(hp == c)(send_gn[2 + c].start)
        for c in range(3):
            pl.when(hp == 2 * c + 1)(functools.partial(small_step, 3 + c))
        return carry

    lax.fori_loop(0, PAIRS, own_step, 0)

    def first_back_product(c, carry):
        cols = pl.ds(pl.multiple_of(c * wide, wide), wide)
        slots[GNT, :, cols] = dot_nt(qkv[...], wqkv[cols, :])
        return carry

    sums_copy(1).start()
    lax.fori_loop(0, D // wide, first_back_product, 0)
    gain_one = row(ln1_gain)

    def first_back(t, carry):
        here = tile(t)
        unit, inverse = unit_of(tok[here, :].astype(f32))
        upstream = slots[GNT, here, :] + gn_in[here, :].astype(f32)
        scaled = upstream * gain_one
        grad = slots[RES, here, :] + inverse * (
            scaled
            - jnp.mean(scaled, axis=1, keepdims=True)
            - unit * jnp.mean(scaled * unit, axis=1, keepdims=True)
        )
        gm[here, :] = grad.astype(bf16)
        return carry

    last_tick = STARTS[-1] + ENDS[-1]
    middle = STARTS[-1] + 2

    def late_ticks(low, high):
        def step(number, carry):
            tick(number, low, high)
            for i, since in enumerate(SUMS_AT):
                if low <= STARTS[-1] + since <= high:
                    pl.when(number == STARTS[-1] + since)(functools.partial(sums_step, 1 + i))
            return carry

        lax.fori_loop(low, high + 1, step, 0)

    late_ticks(STARTS[-1] + 1, middle)
    for copy in send_gn:
        copy.wait()
    lax.fori_loop(0, row_tiles, first_back, 0)
    store_gtok = pltpu.make_async_copy(gm, gtok_hbm.at[0], load_sem.at[2])
    store_gtok.start()
    late_ticks(middle + 1, last_tick)

    me = seq * 2 + blk
    low_row = me * 24 // 16 * 16
    weights = wqkv[pl.ds(pl.multiple_of(low_row, 16), 32), :].astype(f32)
    weights = jnp.where(me * 24 == low_row, weights[:24], weights[8:])
    sums = cs_ref[STAGES]
    lanes = lax.broadcasted_iota(jnp.int32, (24, D), 1)
    mine = lanes == me * 24 + lax.broadcasted_iota(jnp.int32, (24, D), 0)

    def my_column(values):
        return jnp.sum(jnp.where(mine, values, 0.0), axis=1, keepdims=True)

    gain_mine, bias_mine = my_column(row(ln1_gain)), my_column(row(ln1_bias))
    gain_sum = jnp.zeros((24, 1), f32)
    bias_sum = jnp.zeros((24, 1), f32)
    for kind in range(3):
        cols = slice(kind * D, (kind + 1) * D)
        product = out_qkv[:, cols]
        total = sums[kind : kind + 1, :]
        gain_sum += jnp.sum(weights[:, cols] * product, axis=1, keepdims=True)
        bias_sum += jnp.sum(weights[:, cols] * total, axis=1, keepdims=True)
        out_qkv[:, cols] = gain_mine * product + bias_mine * total
    diagonal = lax.broadcasted_iota(jnp.int32, (24, 128), 0) == lax.broadcasted_iota(
        jnp.int32, (24, 128), 1
    )
    for ref, values in (
        (out_ln1g, gain_sum),
        (out_ln1b, bias_sum),
        (out_qb, my_column(sums[0:1])),
        (out_vb, my_column(sums[2:3])),
    ):
        ref[...] = column_sum(jnp.where(diagonal, values, 0.0))[0, :24]
    store_gtok.wait()


def hand_on(*refs):
    for i in range(15):
        refs[15 + i][...] = refs[i][...]


def block_body(
    tokens,
    lengths,
    padding,
    cotangent,
    ln1_gain,
    ln1_bias,
    w_qkv,
    q_bias,
    v_bias,
    w_out,
    out_bias,
    ln2_gain,
    ln2_bias,
    w_fc1,
    fc1_bias,
    w_fc2,
    fc2_bias,
):
    rows = tokens.shape[1]
    n_dev = lax.axis_size("seq") * lax.axis_size("blk")
    shape = jax.ShapeDtypeStruct
    any_spec = pl.BlockSpec(memory_space=pl.ANY)
    vmem = pl.BlockSpec(memory_space=pltpu.VMEM)
    smem = pl.BlockSpec(memory_space=pltpu.SMEM)
    part = D // n_dev
    line = shape((part,), f32)
    outs = pl.pallas_call(
        block_kernel,
        name="block",
        out_shape=(
            shape((1, rows, D), bf16),
            shape((1, rows, D), bf16),
            line,
            line,
            shape((part, 3 * D), f32),
            line,
            line,
            shape((part, D), f32),
            line,
            line,
            line,
            shape((part, FF), f32),
            shape((FF // n_dev,), f32),
            shape((FF // n_dev, D), f32),
            line,
            shape((PAIRS, 2, rows, rows), bf16),
        ),
        in_specs=[
            any_spec, smem, vmem, any_spec, vmem, vmem, any_spec, vmem, vmem,
            any_spec, vmem, vmem, vmem, any_spec, vmem, any_spec, vmem,
        ],
        out_specs=(any_spec,) * 2 + (vmem,) * 13 + (any_spec,),
        scratch_shapes=[
            pltpu.VMEM((D, 3 * D), bf16),
            pltpu.VMEM((D, D), bf16),
            pltpu.VMEM((D, FF), bf16),
            pltpu.VMEM((rows, D), bf16),
            pltpu.VMEM((rows, D), bf16),
            pltpu.VMEM((rows, D), bf16),
            pltpu.VMEM((rows, D), bf16),
            pltpu.VMEM((D, 2 * rows), bf16),
            pltpu.VMEM((D, rows), bf16),
            pltpu.VMEM((rows, 3 * D), bf16),
            pltpu.VMEM((rows, 2 * D), bf16),
            pltpu.VMEM((rows, D), bf16),
            pltpu.VMEM((rows, rows), f32),
            pltpu.VMEM((PAIRS, 2, rows, rows), bf16),
            pltpu.VMEM((7, rows, D), f32),
            pltpu.VMEM((ITEMS * ITEM_ROWS, ITEM_LANES), bf16),
            pltpu.VMEM((SLOTS * LANDING_ROWS, ITEM_LANES), bf16),
            pltpu.VMEM((rows, D), bf16),
            pltpu.VMEM((2, 8, rows), jnp.int32),
            pltpu.VMEM((8, D), f32),
            pltpu.VMEM((8, FF), f32),
            pltpu.VMEM((ITEM_ROWS, 128), f32),
            pltpu.VMEM((LANDING_ROWS, 128), f32),
            pltpu.VMEM((STAGES + 1, 8, D), f32),
            pltpu.VMEM((STAGES, 8, D), f32),
            pltpu.SemaphoreType.DMA((6,)),
            pltpu.SemaphoreType.DMA((PAIRS,)),
            pltpu.SemaphoreType.DMA((9,)),
            pltpu.SemaphoreType.DMA((9,)),
            pltpu.SemaphoreType.DMA((SLOTS * STAGES * len(GROUPS),)),
            pltpu.SemaphoreType.DMA((SLOTS * STAGES * len(GROUPS),)),
            pltpu.SemaphoreType.DMA((STAGES,)),
            pltpu.SemaphoreType.DMA((STAGES,)),
            pltpu.SemaphoreType.DMA((STAGES,)),
            pltpu.SemaphoreType.DMA((STAGES,)),
        ],
        compiler_params=pltpu.CompilerParams(
            collective_id=0, has_side_effects=True, vmem_limit_bytes=VMEM_LIMIT
        ),
        cost_estimate=pl.CostEstimate(
            flops=30 * 10**9, bytes_accessed=60 * 10**6, transcendentals=10**7
        ),
    )(
        tokens, lengths, padding, cotangent, ln1_gain, ln1_bias, w_qkv, q_bias, v_bias,
        w_out, out_bias, ln2_gain, ln2_bias, w_fc1, fc1_bias, w_fc2, fc2_bias,
    )
    return pl.pallas_call(
        hand_on,
        name="hand_on",
        out_shape=tuple(shape(o.shape, o.dtype) for o in outs[:15]),
        in_specs=[vmem] * 15,
        out_specs=(vmem,) * 15,
    )(*outs[:15])


VMEM_LIMIT = 63 * 2**20


def solution(mesh):
    in_specs = (
        P("seq", "blk", None),
        P("seq", None),
        P("seq", "blk"),
        P("seq", "blk", None),
        P(),
        P(),
        P(),
        P(),
        P(),
        P(),
        P(),
        P(),
        P(),
        P(),
        P(),
        P(),
        P(),
    )
    out_specs = (
        P("seq", "blk", None),
        P("seq", "blk", None),
        P(("seq", "blk")),
        P(("seq", "blk")),
        P(("seq", "blk"), None),
        P(("seq", "blk")),
        P(("seq", "blk")),
        P(("seq", "blk"), None),
        P(("seq", "blk")),
        P(("seq", "blk")),
        P(("seq", "blk")),
        P(("seq", "blk"), None),
        P(("seq", "blk")),
        P(("seq", "blk"), None),
        P(("seq", "blk")),
    )
    step = block_body if fits(mesh) else body
    return jax.shard_map(step, mesh=mesh, in_specs=in_specs, out_specs=out_specs, check_vma=False)
```

profile of v0, /device:TPU:0, one launch (start us, length us, event | category | flops | bytes accessed | tf_op | source)
XLA Modules:
  0.0 118.2 jit_solution(5778308858319701603)
XLA Ops:
  0.7 114.2 %block.1 = (bf16[1,512,768]{2,1,0:T(8,128)(2,1)}, bf16[1,512,768]{2,1,0:T(8,128)(2,1)}, f32[24]{0:T(128)}, f32[24]{0:T(128)}, f32[24,2304]{1,0:T(8,128)}, /*inde...) custom-call(bf16[1,512,768]{2,1,0:T(8,128)(2,1)} %tok_hbm.1, ...), custom_call_target="tpu_custom_call" | custom-call | flops 30000001024 | bytes 60000000 | tf_op jit(solution)/shard_map/block/pallas_call | solution.py:1252
  114.9 3.2 %hand_on.1 = (bf16[1,512,768]{2,1,0:T(8,128)(2,1)}, bf16[1,512,768]{2,1,0:T(8,128)(2,1)}, f32[24]{0:T(128)}, f32[24]{0:T(128)}, f32[24,2304]{1,0:T(8,128)}, /*in...) custom-call(bf16[1,512,768]{2,1,0:T(8,128)(2,1)} %get-tuple-element., ...), custom_call_target="tpu_custom_call" | custom-call | tf_op jit(solution)/shard_map/hand_on/pallas_call | solution.py:1325
where the time goes:
time: 118 us
  Pallas kernels  117 us (99%)
    pallas_call x1, Pallas kernels, block_body(): pl.pallas_call(block_kernel, name='block', out_shape=(shape((1, rows, D),...  114 us
    pallas_call x1, Pallas kernels, block_body(): pl.pallas_call(hand_on, name='hand_on', out_shape=tuple((shape(o.shape, o...  3.18 us

commit v1 on v0

--- a/solution.py
+++ b/solution.py
@@ -368,7 +368,7 @@
 PAIRS = HEADS // 2
 FF_CHUNK = 512
 ROW_TILE = 128
-TWIN_UNROLL = 1
+TWIN_UNROLL = 3
 ITEMS = 18
 ITEM_ROWS = 512
 ITEM_LANES = 768
@@ -381,8 +381,9 @@
 LANDING_ROWS = 496
 FLAT_BITS = ("y", "c", "x", "z0", "z1")
 GROUPS = (
-    (("c", "x", "y", "z0", "z1"), 0, 512),
-    (("c", "z0", "z1", "y", "x"), 512, 256),
+    (("c", "x", "y", "z0", "z1"), 0, 384),
+    (("c", "z0", "z1", "y", "x"), 384, 256),
+    (("c", "y", "x", "z0", "z1"), 640, 128),
 )
 
 
@@ -440,19 +441,11 @@
     fc2_bias,
     result_hbm,
     gtok_hbm,
-    out_ln1g,
-    out_ln1b,
     out_qkv,
-    out_qb,
-    out_vb,
     out_out,
-    out_ob,
-    out_ln2g,
-    out_ln2b,
     out_fc1,
-    out_fb1,
     out_fc2,
-    out_fb2,
+    out_small,
     e_hbm,
     wqkv,
     wout,
@@ -528,7 +521,7 @@
             )
         )
     ]
-    for copy in loads:
+    for copy in loads[:2]:
         copy.start()
 
     ends = []
@@ -732,6 +725,8 @@
     first_norm(tok, 0, 0, row_tiles)
     set_bias(True, 0, rows)
     loads[1].wait()
+    for copy in loads[2:]:
+        copy.start()
     wide = 256
 
     def project(kind, add, scale, dst, dst_at, first=0, count=rows):
@@ -832,6 +827,9 @@
 
     forward_three(0)
 
+    def chunk_rows(first, c):
+        return pl.ds(pl.multiple_of(first + c * FF_CHUNK, FF_CHUNK), FF_CHUNK)
+
     send_tags.wait()
     for part in (1, 2):
         first = (part - 1) * part_rows
@@ -847,26 +845,18 @@
 
     loads[2].wait()
 
-    def branch(c, carry):
-        cols = pl.ds(pl.multiple_of(c * wide, wide), wide)
-        out = dot(slots[MIXED].astype(bf16), wout[:, cols])
-        out = out + out_bias[cols].reshape(1, wide)
-        slots[RES, :, cols] = tok[:, cols].astype(f32) + out
-        return carry
-
-    lax.fori_loop(0, D // wide, branch, 0)
     gain_two, offset_two = row(ln2_gain), row(ln2_bias)
-
-    def second_norm(t, carry):
-        unit, _ = unit_of(slots[RES, tile(t), :])
+    for part in range(2):
+        here = slice(part * part_rows, (part + 1) * part_rows)
+        out = dot(slots[MIXED, here, :].astype(bf16), wout[...])
+        residual = tok[here, :].astype(f32) + out + row(out_bias)
+        unit, _ = unit_of(residual)
         normed = (unit * gain_two + offset_two).astype(bf16)
-        nrm[tile(t), :] = normed
-        nrm2_t[:, tile(t)] = normed.T
-        slots[ACC, tile(t), :] = jnp.zeros((ROW_TILE, D), f32)
-        slots[GNT, tile(t), :] = jnp.zeros((ROW_TILE, D), f32)
-        return carry
-
-    lax.fori_loop(0, row_tiles, second_norm, 0)
+        nrm[here, :] = normed
+        nrm2_t[:, here] = normed.T
+        slots[RES, here, :] = residual
+        slots[ACC, here, :] = residual + row(fc2_bias)
+        slots[GNT, here, :] = jnp.zeros((part_rows, D), f32)
 
     loads[3].wait()
     loads[4].wait()
@@ -875,7 +865,7 @@
     def feed(c, carry):
         units = pl.ds(pl.multiple_of(c * FF_CHUNK, FF_CHUNK), FF_CHUNK)
         w1 = wfc1[:, units]
-        w2 = terms[pl.ds(pl.multiple_of(wfc2_at + c * FF_CHUNK, FF_CHUNK), FF_CHUNK), :]
+        w2 = terms[chunk_rows(wfc2_at, c), :]
         pre = dot(nrm[...], w1) + fc1_bias[units].reshape(1, FF_CHUNK)
         phi = 0.5 * (1.0 + lax.erf(pre * 0.7071067811865476))
         slope = phi + pre * jnp.exp(-0.5 * pre * pre) * 0.3989422804014327
@@ -883,19 +873,7 @@
         grad_pre = (dot_nt(cot[...], w2) * slope).astype(bf16)
         slots[ACC] += dot(activated, w2)
         slots[GNT] += dot_nt(grad_pre, w1)
-        @pl.when(c < 4)
-        def _():
-            wqkv[:rows, units] = activated
-
-        @pl.when(c == 4)
-        def _():
-            wqkv[:rows, 8 * wide : 9 * wide] = activated[:, :wide]
-            gm[:, :wide] = activated[:, wide:]
-
-        @pl.when(c == 5)
-        def _():
-            gm[:, wide:] = activated
-
+        terms[chunk_rows(wfc2_at, c), :FF_CHUNK] = activated
         fb1_ref[0:1, units] = column_sum(grad_pre.astype(f32))
         put_24(c, dot(nrm2_t[...], grad_pre))
         feed_tick(c)
@@ -903,13 +881,16 @@
 
     lax.fori_loop(0, FF // FF_CHUNK, feed, 0)
 
-    def weight_fc2(c, activated):
-        values = jnp.concatenate(
-            [dot_tn(activated[:, p * wide : (p + 1) * wide], cot[...]) for p in range(3)], axis=0
-        )
+    def weight_fc2(c, carry):
+        pieces = []
+        for p in range(3):
+            piece = 3 * c + p
+            lanes = pl.ds(pl.multiple_of(lax.rem(piece, 2) * wide, wide), wide)
+            pieces.append(dot_tn(terms[chunk_rows(wfc2_at, piece // 2), lanes], cot[...]))
+        values = jnp.concatenate(pieces, axis=0)
         for low in range(8):
             there = bits_of(low)
-            there["z0"], there["z1"] = (c % 2, c // 2) if isinstance(c, int) else (lax.rem(c, 2), c // 2)
+            there["z0"], there["z1"] = lax.rem(c, 2), c // 2
             for order, lane, width in GROUPS:
                 place = 16 * place_of(order, there)
                 for j in range(6):
@@ -917,16 +898,10 @@
                     block = values[top : top + 16, lane : lane + width].astype(bf16)
                     at = pl.multiple_of((6 + j) * ITEM_ROWS + place, 16)
                     terms[pl.ds(at, 16), lane : lane + width] = block
-
-    def weight_fc2_step(c, carry):
-        weight_fc2(c, wqkv[:rows, pl.ds(pl.multiple_of(c * D, D), D)])
+        pl.when(c == 1)(functools.partial(tick, 6))
         return carry
 
-    lax.fori_loop(0, 3, weight_fc2_step, 0)
-    tick(6)
-    weight_fc2(3, gm[...])
-    reload = pltpu.make_async_copy(wqkv_hbm, wqkv, load_sem.at[1])
-    reload.start()
+    lax.fori_loop(0, 4, weight_fc2, 0)
     tick(7)
 
     vec_ref[...] = jnp.zeros(vec_ref.shape, f32)
@@ -940,9 +915,7 @@
     def second_back(t, carry):
         here = tile(t)
         unit, inverse = unit_of(slots[RES, here, :])
-        tokp[here, :] = (
-            slots[RES, here, :] + slots[ACC, here, :] + row(fc2_bias)
-        ).astype(bf16)
+        tokp[here, :] = slots[ACC, here, :].astype(bf16)
         upstream = slots[GNT, here, :]
         grad_out = cot[here, :].astype(f32)
         add_vec(V_FC2B, grad_out)
@@ -1011,9 +984,7 @@
         if stage < STAGES:
             small_copy(stage + 1).start()
             return
-        for kind, ref in enumerate((out_ob, out_ln2g, out_ln2b, out_fb2)):
-            ref[...] = small[kind, :24]
-        out_fb1[...] = small[8, :96]
+        out_small[:9, :] = small[:9, :]
 
     small_copy(1).start()
 
@@ -1077,7 +1048,6 @@
             qkv[:, cols] = total_q.astype(bf16)
 
     store_result.wait()
-    reload.wait()
     send_gn = []
     for part in (1, 2):
         first = (part - 1) * part_rows
@@ -1146,7 +1116,6 @@
         return carry
 
     sums_copy(1).start()
-    lax.fori_loop(0, D // wide, first_back_product, 0)
     gain_one = row(ln1_gain)
 
     def first_back(t, carry):
@@ -1162,26 +1131,33 @@
         gm[here, :] = grad.astype(bf16)
         return carry
 
-    last_tick = STARTS[-1] + ENDS[-1]
-    middle = STARTS[-1] + 2
-
-    def late_ticks(low, high):
-        def step(number, carry):
-            tick(number, low, high)
-            for i, since in enumerate(SUMS_AT):
-                if low <= STARTS[-1] + since <= high:
-                    pl.when(number == STARTS[-1] + since)(functools.partial(sums_step, 1 + i))
-            return carry
-
-        lax.fori_loop(low, high + 1, step, 0)
-
-    late_ticks(STARTS[-1] + 1, middle)
-    for copy in send_gn:
-        copy.wait()
-    lax.fori_loop(0, row_tiles, first_back, 0)
     store_gtok = pltpu.make_async_copy(gm, gtok_hbm.at[0], load_sem.at[2])
-    store_gtok.start()
-    late_ticks(middle + 1, last_tick)
+    last_start = STARTS[-1]
+    product_at = last_start + 1
+    tokens_at = product_at + D // wide
+
+    def late_tick(number, carry):
+        tick(number, last_start + 1, last_start + ENDS[-1])
+        for i, since in enumerate(SUMS_AT):
+            pl.when(number == last_start + since)(functools.partial(sums_step, 1 + i))
+
+        @pl.when(number < tokens_at)
+        def _():
+            first_back_product(number - product_at, 0)
+
+        @pl.when(number == tokens_at)
+        def _():
+            for copy in send_gn:
+                copy.wait()
+
+        @pl.when((number >= tokens_at) & (number < tokens_at + row_tiles))
+        def _():
+            first_back(number - tokens_at, 0)
+
+        pl.when(number == tokens_at + row_tiles)(store_gtok.start)
+        return carry
+
+    lax.fori_loop(last_start + 1, last_start + ENDS[-1] + 1, late_tick, 0)
 
     me = seq * 2 + blk
     low_row = me * 24 // 16 * 16
@@ -1207,19 +1183,24 @@
     diagonal = lax.broadcasted_iota(jnp.int32, (24, 128), 0) == lax.broadcasted_iota(
         jnp.int32, (24, 128), 1
     )
-    for ref, values in (
-        (out_ln1g, gain_sum),
-        (out_ln1b, bias_sum),
-        (out_qb, my_column(sums[0:1])),
-        (out_vb, my_column(sums[2:3])),
+    for kind, values in enumerate(
+        (gain_sum, bias_sum, my_column(sums[0:1]), my_column(sums[2:3]))
     ):
-        ref[...] = column_sum(jnp.where(diagonal, values, 0.0))[0, :24]
+        line = column_sum(jnp.where(diagonal, values, 0.0))
+        out_small[9 + kind : 10 + kind, :] = line
     store_gtok.wait()
 
 
+SMALL_ROWS = ((2, 9), (3, 10), (5, 11), (6, 12), (8, 0), (9, 1), (10, 2), (12, 8), (14, 3))
+LARGE = (0, 1, 4, 7, 11, 13)
+
+
 def hand_on(*refs):
-    for i in range(15):
-        refs[15 + i][...] = refs[i][...]
+    large, small, outs = refs[:6], refs[6], refs[7:22]
+    for ref, at in zip(large, LARGE):
+        outs[at][...] = ref[...]
+    for at, line in SMALL_ROWS:
+        outs[at][...] = small[line, : outs[at].shape[0]]
 
 
 def block_body(
@@ -1255,26 +1236,18 @@
         out_shape=(
             shape((1, rows, D), bf16),
             shape((1, rows, D), bf16),
-            line,
-            line,
             shape((part, 3 * D), f32),
-            line,
-            line,
             shape((part, D), f32),
-            line,
-            line,
-            line,
             shape((part, FF), f32),
-            shape((FF // n_dev,), f32),
             shape((FF // n_dev, D), f32),
-            line,
+            shape((16, 128), f32),
             shape((PAIRS, 2, rows, rows), bf16),
         ),
         in_specs=[
             any_spec, smem, vmem, any_spec, vmem, vmem, any_spec, vmem, vmem,
             any_spec, vmem, vmem, vmem, any_spec, vmem, any_spec, vmem,
         ],
-        out_specs=(any_spec,) * 2 + (vmem,) * 13 + (any_spec,),
+        out_specs=(any_spec,) * 2 + (vmem,) * 5 + (any_spec,),
         scratch_shapes=[
             pltpu.VMEM((D, 3 * D), bf16),
             pltpu.VMEM((D, D), bf16),
@@ -1322,13 +1295,17 @@
         tokens, lengths, padding, cotangent, ln1_gain, ln1_bias, w_qkv, q_bias, v_bias,
         w_out, out_bias, ln2_gain, ln2_bias, w_fc1, fc1_bias, w_fc2, fc2_bias,
     )
+    final = (
+        outs[0], outs[1], line, line, outs[2], line, line, outs[3], line, line, line, outs[4],
+        shape((FF // n_dev,), f32), outs[5], line,
+    )
     return pl.pallas_call(
         hand_on,
         name="hand_on",
-        out_shape=tuple(shape(o.shape, o.dtype) for o in outs[:15]),
-        in_specs=[vmem] * 15,
+        out_shape=tuple(shape(o.shape, o.dtype) for o in final),
+        in_specs=[vmem] * 7,
         out_specs=(vmem,) * 15,
-    )(*outs[:15])
+    )(*outs[:7])
 
 
 VMEM_LIMIT = 63 * 2**20

time: 118 us -> 117 us (level)
    pallas_call x1, Pallas kernels: 114 us -> 113 us  [block_body(): pl.pallas_call(block_kernel, name='block', out_shape=(shape((1, rows, D),...]
where the time goes in v1:
time: 117 us; the launch traced here: 116 us
  Pallas kernels  116 us (99%)
    pallas_call x1, Pallas kernels, block_body(): pl.pallas_call(block_kernel, name='block', out_shape=(shape((1, rows, D),...  113 us
    pallas_call x1, Pallas kernels, block_body(): pl.pallas_call(hand_on, name='hand_on', out_shape=tuple((shape(o.shape, o...  3.14 us

profile of v1, /device:TPU:0, one launch (start us, length us, event | category | flops | bytes accessed | tf_op | source)
XLA Modules:
  0.0 116.5 jit_solution(10456278091494305143)
XLA Ops:
  0.7 112.5 %block.1 = (bf16[1,512,768]{2,1,0:T(8,128)(2,1)}, bf16[1,512,768]{2,1,0:T(8,128)(2,1)}, f32[24,2304]{1,0:T(8,128)}, f32[24,768]{1,0:T(8,128)}, f32[24,3072]{1,0:...) custom-call(bf16[1,512,768]{2,1,0:T(8,128)(2,1)} %tok_hbm.1, s32[1,4]{1,0:T(1,128)} %len_ref.1, ...), custom_call_target="tpu_custom_call" | custom-call | flops 30000001024 | bytes 60000000 | tf_op jit(solution)/shard_map/block/pallas_call | solution.py:1233
  113.2 3.1 %hand_on.1 = (bf16[1,512,768]{2,1,0:T(8,128)(2,1)}, bf16[1,512,768]{2,1,0:T(8,128)(2,1)}, f32[24]{0:T(128)}, f32[24]{0:T(128)}, f32[24,2304]{1,0:T(8,128)}, /*in...) custom-call(bf16[1,512,768]{2,1,0:T(8,128)(2,1)} %get-tuple-element., ...), custom_call_target="tpu_custom_call" | custom-call | tf_op jit(solution)/shard_map/hand_on/pallas_call | solution.py:1302
